TPU v7x, 32 devices: a whole 2x2x4 slice. The times are simulated.
32 devices in a mesh: fields: 2 (over x), prow: 8 (over z, y), pcol: 2 (over core).
Axes of the slice: x: 2, y: 2, z: 4, core: 2. Of those that a mesh axis runs over, the one named last changes fastest.
Arguments:
- inverse_tiles: bfloat16 [32, 16, 256, 256], P(('fields', 'prow'), 'pcol'), parts along dimension 0, may hold values from -6 to 6
- panel_blocks: bfloat16 [4, 8, 256, 512], P('fields', 'prow', None, 'pcol'), parts along dimension 0, may hold values from -0.125 to 0.125
- diag_inverse: float32 [4, 512], P('fields', 'pcol'), parts along dimension 0, may hold values from 0.5 to 2
- structure: int32 [4, 8], P('fields'), parts along dimension 0, may hold values from 0 to 15, as said below
- block_slot: int32 [32], P('fields'), parts along dimension 0, may hold values from 0 to 15, each once
Outputs:
- sigma_new: bfloat16 [4, 16, 256, 512], P('fields', 'prow', None, 'pcol'), parts along dimension 0
- variances: float32 [4, 512], P('fields', 'pcol'), parts along dimension 0
There are 2 independent parts, one for each index of `fields`. A program takes and returns all parts, laid end to end along the dimension named above; each array names one. Nothing has to cross between parts.
Inputs may be any that keep to these rules, and one draw needn't show every extreme that they name: `structure`: each row lists 8 distinct row blocks in increasing order, and the last is always 16 - 1. `block_slot`: each slot is used by exactly one row block.
All inputs are finite; a program needn't handle non-finite values.
Results may differ from a plain program's by a relative error of at most 0.0006.
Values may be sent and summed in bfloat16 or wider, within the bound.
A program may use at most 128 MiB of HBM per device.

v0:
```python
import jax
import jax.numpy as jnp
from jax import lax
from jax.sharding import PartitionSpec as P


def swapped(shard, axis, stride):
    return lax.ppermute(shard, axis, [(i, i ^ 1 << stride) for i in range(lax.axis_size(axis))])


def make_accumulate(selected, row_hits, piece):
    contrib = jnp.einsum("iskxy,skyw->sixw", selected, piece, preferred_element_type=jnp.float32)
    own_panel = jnp.einsum("sik,skxw->sixw", row_hits, piece, preferred_element_type=jnp.float32)
    return (contrib, own_panel)


def per_device(inverse_tiles, panel_blocks, diag_inverse, structure, block_slot):
    rows_here = inverse_tiles.shape[0]
    tile_size = inverse_tiles.shape[2]
    supernodes = panel_blocks.shape[0]
    positions = structure.shape[1]
    prow_index = lax.axis_index("prow")
    pcol_index = lax.axis_index("pcol")
    slot_of = block_slot[structure]
    own_rows = prow_index * rows_here + jnp.arange(rows_here, dtype=jnp.int32)
    row_match = slot_of[:, None, :] == own_rows[None, :, None]
    row_hits = row_match.astype(jnp.bfloat16)
    row_used = jnp.any(row_match, axis=2)
    partner = swapped(inverse_tiles, "pcol", 0)
    first_half = jnp.where(pcol_index == 0, inverse_tiles, partner)
    second_half = jnp.where(pcol_index == 0, partner, inverse_tiles)
    whole_rows = jnp.concatenate([first_half, second_half], axis=1)
    selected = jnp.take(whole_rows, slot_of.reshape(-1), axis=1)
    selected = selected.reshape(rows_here, supernodes, positions, tile_size, tile_size)
    summed, own_panel = make_accumulate(
        selected, row_hits, lax.all_gather(panel_blocks, "prow", axis=1, tiled=True)
    )
    sigma_rows = jnp.where(row_used[:, :, None, None], -summed, jnp.zeros((), jnp.float32))
    partial_value = jnp.sum(own_panel * sigma_rows, axis=(1, 2))
    correction = lax.psum(partial_value, "prow")
    variances = diag_inverse - correction
    return (sigma_rows.astype(jnp.bfloat16), variances)


def solution(mesh):
    in_specs = (
        P(("fields", "prow"), "pcol", None, None),
        P("fields", "prow", None, "pcol"),
        P("fields", "pcol"),
        P("fields", None),
        P("fields"),
    )
    out_specs = (P("fields", "prow", None, "pcol"), P("fields", "pcol"))
    return jax.shard_map(
        per_device, mesh=mesh, in_specs=in_specs, out_specs=out_specs, check_vma=False
    )
```

profile of v0, /device:TPU:0, one launch (start us, length us, event | category | flops | bytes accessed | tf_op | source)
XLA Modules:
  0.0 96.1 jit_solution(17099047433927221169)
XLA Ops:
  7.2 0.0 copy-start
  7.2 0.0 all-gather.2.cloned.1.call-start
  7.2 0.7 all-gather.2.cloned.1.call-update
  7.9 0.5 collective-permute-start
  8.4 0.7 compare_select_fusion.1
  9.1 0.1 reshape.53
  9.2 0.0 copy-done
  9.2 0.7 gather_fusion
  9.9 0.1 reshape.52
  10.0 0.2 compare_reduce_fusion
  10.2 2.3 %collective-permute-done = bf16[2,8,256,256]{3,2,1,0:T(8,128)(2,1)S(1)} collective-permute-done((bf16[2,8,256,256]{3,2,1,0:T(8,128)(2,1)}, bf16[2,8,256,256]{3,2,1,0:T(8,128)(2,1)S(1)}, u32[]{:S(2)}, u32[]{:S(2)}) %collective-permute-start) | collective-permute-done | bytes 2097184 | tf_op jit(solution)/shard_map/ppermute | solution.py:8
  12.4 1.9 %broadcast_select_fusion.1 = (bf16[2,8,256,256]{3,2,1,0:T(8,128)(2,1)S(1)}, bf16[2,8,256,256]{3,2,1,0:T(8,128)(2,1)S(1)}) fusion(bf16[2,8,256,256]{3,2,1,0:T(8,128)(2,1)} %param.5, bf16[2,8,256,256]{3,2,1,0:T(8,128)(2,1)S(1)} %collective-permute-done, pred[]{:T(512)S(6)} %eq.20), kind=kLoop, calls=%fused_computation.11 | loop fusion | flops 2097152 | bytes 8388609 | tf_op jit(solution)/shard_map/jit(_where)/select_n | solution.py:30
  14.3 2.3 %pad_maximum_fusion = bf16[2,16,256,256]{3,2,1,0:T(8,128)(2,1)} fusion(bf16[2,8,256,256]{3,2,1,0:T(8,128)(2,1)S(1)} %get-tuple-element.3, bf16[2,8,256,256]{3,2,1,0:T(8,128)(2,1)S(1)} %get-tuple-element.2), kind=kLoop, calls=%fused_computation.2 | loop fusion | flops 2097152 | bytes 8388608 | tf_op jit(solution)/shard_map/concatenate | solution.py:32
  16.6 4.9 %gather_fusion.1 = bf16[16,2,256,256]{3,2,1,0:T(8,128)(2,1)} fusion(bf16[2,16,256,256]{3,2,1,0:T(8,128)(2,1)} %pad_maximum_fusion, s32[1024]{0:T(1024)S(1)} %pad_clamp_fusion), kind=kCustom, calls=%fused_computation.1 | custom fusion | bytes 8388672 | tf_op jit(solution)/shard_map/jit(_take)/gather | solution.py:33
  21.6 40.6 %all-gather.2.cloned.1.call-done = bf16[2,8,256,256]{3,2,1,0:T(8,128)(2,1)} async-done(((bf16[2,1,256,256]{3,2,1,0:T(8,128)(2,1)}), bf16[2,8,256,256]{3,2,1,0:T(8,128)(2,1)}) %all-gather.2.cloned.1.call-update) | async-done | bytes 2097168 | tf_op jit(solution)/shard_map/all_gather | solution.py:36
  62.2 0.0 copy-start.1
  62.2 3.2 %fusion.3 = f32[2,2,256,256]{3,1,2,0:T(2,128)S(1)} fusion(bf16[2,8,256,256]{3,2,1,0:T(8,128)(2,1)} %all-gather.2.cloned.1.call-done, s32[2,8]{1,0:T(2,128)S(1)} %reshape.52, s32[2]{0:T(128)S(1)} %iota_add_fusion), kind=kOutput, calls=%fused_computation.7 | convolution fusion | flops 4194336 | bytes 3145800 | tf_op jit(solution)/shard_map/sik,skxw->sixw/dot_general | solution.py:13
  65.4 0.0 copy-done.1
  65.4 0.0 copy-start.2
  65.4 4.3 %fusion.15 = (f32[2,256]{1,0:T(2,128)S(1)}, bf16[2,2,256,256]{3,2,1,0:T(8,128)(2,1)}) fusion(f32[2,2,256,256]{3,1,2,0:T(2,128)S(1)} %fusion.3, bf16[2,8,256,256]{3,2,1,0:T(8,128)(2,1)S(1)} %copy-done.1, bf16[2,2,8,256,256]{4,3,0,2,1:T(8,128)(2,1)} %bitcast.32, pred[2,8]{1,0:T(4,128)(4,1)S(1)} %compare_and_fusion, pred[2,2]{1,0:T(4,128)(4,1)S(1)} %compare_reduce_fusion), kind=kOutput, calls=%fused_computation.16 | convolution fusion | flops 1077149184 | bytes 7866388 | tf_op jit(solution)/shard_map/iskxy,skyw->sixw/dot_general | solution.py:12
  69.7 18.9 %psum.7 = f32[2,256]{1,0:T(2,128)S(1)} all-reduce(f32[2,256]{1,0:T(2,128)S(1)} %get-tuple-element.4), channel_id=1, replica_groups=mesh['fields'=2,'prow'=8,'pcol'=2] {'prow'}, use_global_device_ids=true, to_apply=%region_2.3 | all-reduce | flops 512 | bytes 4096 | tf_op jit(solution)/shard_map/psum | solution.py:40
  88.6 0.0 copy-done.2
  88.6 0.6 sub.3
  (5 shorter events, 0.0 us)
Async XLA Ops:
  7.2 2.0 %copy-start = (s32[16]{0:T(128)S(1)}, s32[16]{0:T(128)}, u32[]{:S(2)}) copy-start(s32[16]{0:T(128)} %param.9) | copy-start | bytes 196
  7.2 55.0 %all-gather.2.cloned.1.call-start = ((), (), s32[]{:S(2)}) async-start(), calls=%async_computation | async-start | bytes 2359296 | tf_op jit(solution)/shard_map/all_gather | solution.py:36
  7.9 4.5 %collective-permute-start = (bf16[2,8,256,256]{3,2,1,0:T(8,128)(2,1)}, bf16[2,8,256,256]{3,2,1,0:T(8,128)(2,1)S(1)}, u32[]{:S(2)}, u32[]{:S(2)}) collective-permute-start(bf16[2,8,256,256]{3,2,1,0:T(8,128)(2,1)} %param.5), channel_id=1, source_target_pairs={{0,1},{1,0},{2,3},{3,2},{4,5},{5,4},{6,7},{7,6},{8,9},{9,8},{10,11... | collective-permute-start | bytes 6291464 | tf_op jit(solution)/shard_map/ppermute | solution.py:8
  62.2 3.2 %copy-start.1 = (bf16[2,8,256,256]{3,2,1,0:T(8,128)(2,1)S(1)}, bf16[2,8,256,256]{3,2,1,0:T(8,128)(2,1)}, u32[]{:S(2)}) copy-start(bf16[2,8,256,256]{3,2,1,0:T(8,128)(2,1)} %all-gather.2.cloned.1.call-done) | copy-start | bytes 6291460
  65.4 23.2 %copy-start.2 = (f32[2,256]{1,0:T(2,128)S(1)}, f32[2,256]{1,0:T(2,128)}, u32[]{:S(2)}) copy-start(f32[2,256]{1,0:T(2,128)} %param.7) | copy-start | bytes 6148
Sparse Core Ops, SparseCore 0:
  10.2 51.9 all-gather.1
where the time goes:
time: 96.3 us; the launch traced here: 96.1 us
  waiting for transfers between devices  43.6 us (45%)
  blocking collectives  18.9 us (20%)
  between operations  14.1 us (15%)
  matrix products  7.51 us (8%)
  local copies, waits for them, and re-layouts  5.78 us (6%)
  other arithmetic  5.67 us (6%)
    all_gather x1, waiting for transfers between devices, per_device(): lax.all_gather(panel_blocks, 'prow', axis=1, tiled=True)  40.6 us
    psum x1, blocking collectives, per_device(): correction = lax.psum(partial_value, 'prow')  18.9 us
    gather x1, local copies, waits for them, and re-layouts, per_device(): selected = jnp.take(whole_rows, slot_of.reshape(-1), axis=1)  4.94 us
    dot_general x1, matrix products, make_accumulate(): jnp.einsum('iskxy,skyw->sixw', selected, piece, preferred_element_type=jn...  4.32 us
    dot_general x1, matrix products, make_accumulate(): jnp.einsum('sik,skxw->sixw', row_hits, piece, preferred_element_type=jnp....  3.19 us
    concatenate x1, other arithmetic, per_device(): whole_rows = jnp.concatenate([first_half, second_half], axis=1)  2.33 us
    ppermute x1, waiting for transfers between devices, swapped(): lax.ppermute(shard, axis, [(i, i ^ 1 << stride) for i in range(lax.axis_s...  2.26 us
  transfers between devices with their start and end apart: 2, of which 2 were waited for; matrix products, arithmetic and copies ran while one was open for 11% of the time, Pallas kernels for 0%

commit v1 on v0

v1 whole, which is shorter than its diff:
```python
import functools

import jax
import jax.numpy as jnp
from jax import lax
from jax.experimental import pallas as pl
from jax.experimental.pallas import tpu as pltpu
from jax.sharding import PartitionSpec as P

MESH = pl.DeviceIdType.MESH
UP, DOWN, ACROSS, EXTRA = range(4)


def grid_of(mesh):
    count = mesh.shape["prow"]
    line = None
    devices = getattr(mesh, "devices", None)
    if devices is not None and hasattr(devices.flat[0], "coords"):
        line = len({tuple(d.coords)[2] for d in devices[0, :, 0]})
    if line is None and count % 2 == 0:
        line = count // 2
    if line is None or line * 2 != count or line % 2:
        return count, 1
    return line, 2


def kernel(
    line, wide, structure, block_slot, tiles, panel, diag, sigma, variance,
    full, acc, part, parts, *rest,
):
    supers = structure.shape[0]
    positions = structure.shape[1]
    rows, columns, tile = tiles.shape[0], tiles.shape[1], tiles.shape[2]
    width = panel.shape[3]
    held = positions // (line * wide)
    count = line * wide
    panels = rest[:supers]
    (
        panel_sem, send_sem, recv_sem, tile_sem, tile_send, tile_recv,
        part_send, part_recv,
    ) = rest[supers:]

    me = lax.axis_index("prow")
    core = lax.axis_index("pcol")
    z, y = me // wide, me % wide
    sibling = z * wide + (wide - 1 - y)
    twin = (z + 1 - 2 * (z % 2)) * wide + y
    last = supers - 1

    def at(zz, yy):
        return zz * wide + yy

    barrier = pltpu.get_barrier_semaphore()
    for shift in range(1, count):
        pl.semaphore_signal(
            barrier, inc=1, device_id={"prow": lax.rem(me + shift, count)},
            device_id_type=MESH,
        )
    pl.semaphore_signal(barrier, inc=1, device_id={"pcol": 1 - core}, device_id_type=MESH)
    pl.semaphore_wait(barrier, count)

    def send(s, source, kind, to, own=False):
        return pltpu.make_async_remote_copy(
            src_ref=panel.at[s] if own else panels[s].at[source],
            dst_ref=panels[s].at[source],
            send_sem=send_sem.at[kind, s, source],
            recv_sem=recv_sem.at[s, source],
            device_id={"prow": to},
            device_id_type=MESH,
        )

    def arrive(s, source):
        send(s, source, UP, me).wait_recv()

    up, down = at(z + 1, y), at(z - 1, y)
    has_up, has_down = z + 1 < line, z >= 1

    for s in range(supers):
        if wide == 2:
            send(s, me, ACROSS, sibling, True).start()

        @pl.when(has_up)
        def _():
            send(s, me, UP, up, True).start()

        @pl.when(has_down)
        def _():
            send(s, me, DOWN, down, True).start()

    swap = pltpu.make_async_remote_copy(
        src_ref=tiles,
        dst_ref=full.at[:, pl.ds(core * columns, columns)],
        send_sem=tile_send,
        recv_sem=tile_recv,
        device_id={"pcol": 1 - core},
        device_id_type=MESH,
    )
    swap.start()
    keep = pltpu.make_async_copy(
        tiles, full.at[:, pl.ds(core * columns, columns)], tile_sem
    )
    keep.start()
    own = [
        pltpu.make_async_copy(panel.at[s], panels[s].at[me], panel_sem.at[s])
        for s in range(supers)
    ]
    for s in range(supers):
        own[s].start()
    for s in range(supers):
        acc[s] = jnp.zeros(acc.shape[1:], acc.dtype)

    def add(s, source):
        for k in range(held):
            slot = block_slot[structure[s, source * held + k]]
            left = full[:, slot].reshape(rows * tile, tile)
            acc[s] += jnp.dot(
                left, panels[s][source, k], preferred_element_type=jnp.float32
            )

    def crosses(s, zz):
        if s != last:
            return zz >= 0
        return zz != z + 1 - 2 * (z % 2)

    def flush():
        for s in range(supers):
            own[s].wait()
        keep.wait()
        swap.wait_recv()
        for s in range(supers):
            add(s, me)

    def step(d, _):
        above, below = z + d, z - d
        for s in range(supers):
            @pl.when(above < line)
            def _():
                arrive(s, at(above, y))

                @pl.when(has_down)
                def _():
                    send(s, at(above, y), DOWN, down).start()

                if wide == 2:
                    @pl.when(crosses(s, above))
                    def _():
                        send(s, at(above, y), ACROSS, sibling).start()

            @pl.when(below >= 0)
            def _():
                arrive(s, at(below, y))

                @pl.when(has_up)
                def _():
                    send(s, at(below, y), UP, up).start()

                if wide == 2:
                    @pl.when(crosses(s, below))
                    def _():
                        send(s, at(below, y), ACROSS, sibling).start()

            if s == 0:
                @pl.when(d == 1)
                def _():
                    flush()

            @pl.when(above < line)
            def _():
                add(s, at(above, y))

            @pl.when(below >= 0)
            def _():
                add(s, at(below, y))

            if wide == 2:
                across(s, d - 1)
        return 0

    def across(s, d):
        above, below = z + d, z - d

        @pl.when((above < line) & crosses(s, above))
        def _():
            arrive(s, at(above, 1 - y))
            add(s, at(above, 1 - y))

        @pl.when((below >= 0) & crosses(s, below) & (d > 0))
        def _():
            arrive(s, at(below, 1 - y))
            add(s, at(below, 1 - y))

    lax.fori_loop(1, line, step, 0)

    if wide == 2:
        extra = send(last, sibling, EXTRA, twin)
        extra.start()

    def finish(s):
        total = jnp.zeros((1, width), jnp.float32)
        for r in range(rows):
            row = me * rows + r
            position, used = jnp.int32(0), jnp.int32(0)
            for a in range(positions):
                hit = block_slot[structure[s, a]] == row
                position = jnp.where(hit, a, position)
                used = jnp.where(hit, 1, used)
            value = jnp.where(used > 0, -acc[s, r * tile:(r + 1) * tile, :], 0.0)
            sigma[s, r] = value.astype(sigma.dtype)
            mine = panels[s][position // held, position % held].astype(jnp.float32)
            total = total + jnp.sum(mine * value, axis=0, keepdims=True)
        part[s:s + 1, :] = total

    for s in range(supers):
        if wide == 2:
            across(s, line - 1)
            if s == last:
                arrive(s, at(z + 1 - 2 * (z % 2), 1 - y))
                add(s, at(z + 1 - 2 * (z % 2), 1 - y))
        finish(s)

    def share(shift):
        to = lax.rem(me + shift, count)
        return pltpu.make_async_remote_copy(
            src_ref=part,
            dst_ref=parts.at[shift],
            send_sem=part_send.at[shift],
            recv_sem=part_recv.at[shift],
            device_id={"prow": to},
            device_id_type=MESH,
        )

    for shift in range(1, count):
        share(shift).start()

    for s in range(supers):
        if wide == 2:
            send(s, me, ACROSS, sibling, True).wait_send()

        @pl.when(has_up)
        def _():
            send(s, me, UP, up, True).wait_send()

        @pl.when(has_down)
        def _():
            send(s, me, DOWN, down, True).wait_send()

    def left(d, _):
        above, below = z + d, z - d
        for s in range(supers):
            @pl.when(above < line)
            def _():
                @pl.when(has_down)
                def _():
                    send(s, at(above, y), DOWN, down).wait_send()

                if wide == 2:
                    @pl.when(crosses(s, above))
                    def _():
                        send(s, at(above, y), ACROSS, sibling).wait_send()

            @pl.when(below >= 0)
            def _():
                @pl.when(has_up)
                def _():
                    send(s, at(below, y), UP, up).wait_send()

                if wide == 2:
                    @pl.when(crosses(s, below))
                    def _():
                        send(s, at(below, y), ACROSS, sibling).wait_send()
        return 0

    lax.fori_loop(1, line, left, 0)
    if wide == 2:
        extra.wait_send()
    swap.wait_send()

    total = diag[...] - part[...]
    for shift in range(1, count):
        share(shift).wait()
        total = total - parts[shift]
    variance[...] = total


def per_device(line, wide, inverse_tiles, panel_blocks, diag_inverse, structure, block_slot):
    rows, columns, tile, _ = inverse_tiles.shape
    supers, held, _, width = panel_blocks.shape
    count = line * wide
    bf16, f32 = jnp.bfloat16, jnp.float32
    dma = pltpu.SemaphoreType.DMA
    whole = pl.BlockSpec(memory_space=pltpu.VMEM)
    scalars = pl.BlockSpec(memory_space=pltpu.SMEM)
    anywhere = pl.BlockSpec(memory_space=pl.ANY)
    flops = 2 * supers * rows * tile * width * tile * structure.shape[1]
    return pl.pallas_call(
        functools.partial(kernel, line, wide),
        out_shape=(
            jax.ShapeDtypeStruct((supers, rows, tile, width), bf16),
            jax.ShapeDtypeStruct((supers, width), f32),
        ),
        in_specs=[scalars, scalars, anywhere, anywhere, whole],
        out_specs=(whole, whole),
        scratch_shapes=[
            pltpu.VMEM((rows, 2 * columns, tile, tile), bf16),
            pltpu.VMEM((supers, rows * tile, width), f32),
            pltpu.VMEM((supers, width), f32),
            pltpu.VMEM((count, supers, width), f32),
            *[pltpu.VMEM((count, held, tile, width), bf16) for _ in range(supers)],
            dma((supers,)),
            dma((4, supers, count)),
            dma((supers, count)),
            dma,
            dma,
            dma,
            dma((count,)),
            dma((count,)),
        ],
        compiler_params=pltpu.CompilerParams(
            collective_id=0, has_side_effects=True, vmem_limit_bytes=48 * 2**20
        ),
        cost_estimate=pl.CostEstimate(
            flops=flops, bytes_accessed=4 * inverse_tiles.size, transcendentals=0
        ),
    )(structure, block_slot, inverse_tiles, panel_blocks, diag_inverse)


def solution(mesh):
    line, wide = grid_of(mesh)
    in_specs = (
        P(("fields", "prow"), "pcol", None, None),
        P("fields", "prow", None, "pcol"),
        P("fields", "pcol"),
        P("fields", None),
        P("fields"),
    )
    out_specs = (P("fields", "prow", None, "pcol"), P("fields", "pcol"))
    return jax.shard_map(
        functools.partial(per_device, line, wide),
        mesh=mesh, in_specs=in_specs, out_specs=out_specs, check_vma=False,
    )
```

time: 96.3 us -> 42.9 us (0.45)
  waiting for transfers between devices: 43.6 us -> 0 us
  Pallas kernels: 0 us -> 36.1 us
  blocking collectives: 18.9 us -> 0 us
  between operations: 14.1 us -> 0.65 us
  matrix products: 7.51 us -> 0 us
  other arithmetic: 5.67 us -> 0 us
    all_gather x1 -> x0, waiting for transfers between devices: 40.6 us -> none  [per_device(): lax.all_gather(panel_blocks, 'prow', axis=1, tiled=True)]
    pallas_call x0 -> x1, Pallas kernels: none -> 36.1 us  [per_device(): pl.pallas_call(functools.partial(kernel, line, wide), out_shape=(jax.Shap...]
    psum x1 -> x0, blocking collectives: 18.9 us -> none  [per_device(): correction = lax.psum(partial_value, 'prow')]
    dot_general x2 -> x0, matrix products: 7.51 us -> none  [the longest x1 4.32 us: make_accumulate(): jnp.einsum('iskxy,skyw->sixw', selected, piece, preferred_element_type=jn...]
    unnamed x6 -> x12, local copies, waits for them, and re-layouts: 0.02 us -> 5.92 us
    gather x3 -> x0, local copies, waits for them, and re-layouts: 5.68 us -> none  [the longest x1 4.94 us: per_device(): selected = jnp.take(whole_rows, slot_of.reshape(-1), axis=1)]
    select_n x3 -> x0, other arithmetic: 2.55 us -> none  [the longest x1 1.87 us: per_device(): first_half = jnp.where(pcol_index == 0, inverse_tiles, partner)]
    concatenate x1 -> x0, other arithmetic: 2.33 us -> none  [per_device(): whole_rows = jnp.concatenate([first_half, second_half], axis=1)]
  transfers between devices with their start and end apart: 2 -> 0, of which waited for: 2 -> 0; matrix products, arithmetic and copies ran while one was open for 11% -> 0% of each run, Pallas kernels for 0% -> 0%
where the time goes in v1:
time: 42.9 us; the launch traced here: 42.7 us
  Pallas kernels  36.1 us (84%)
  local copies, waits for them, and re-layouts  5.92 us (14%)
  between operations  0.65 us (2%)
    pallas_call x1, Pallas kernels, per_device(): pl.pallas_call(functools.partial(kernel, line, wide), out_shape=(jax.Shap...  36.1 us
    unnamed x12, local copies, waits for them, and re-layouts  5.92 us

profile of v1, /device:TPU:0, one launch (start us, length us, event | category | flops | bytes accessed | tf_op | source)
XLA Modules:
  0.0 42.7 jit_solution(1091773397278479155)
XLA Ops:
  0.6 0.0 copy-start
  0.6 1.6 %copy-done = bf16[2,8,256,256]{3,2,1,0:T(8,128)(2,1)S(1)} copy-done((bf16[2,8,256,256]{3,2,1,0:T(8,128)(2,1)S(1)}, bf16[2,8,256,256]{3,2,1,0:T(8,128)(2,1)}, u32[]{:S(2)}) %copy-start) | copy-done | bytes 2097176
  2.2 0.0 copy-start.1
  2.2 0.9 %copy-done.1 = bf16[2,1,256,256]{3,2,1,0:T(8,128)(2,1)S(1)} copy-done((bf16[2,1,256,256]{3,2,1,0:T(8,128)(2,1)S(1)}, bf16[2,1,256,256]{3,2,1,0:T(8,128)(2,1)}, u32[]{:S(2)}) %copy-start.1) | copy-done | bytes 262168
  3.2 0.0 copy-start.2
  3.2 0.7 %copy-done.2 = f32[2,256]{1,0:T(2,128)S(1)} copy-done((f32[2,256]{1,0:T(2,128)S(1)}, f32[2,256]{1,0:T(2,128)}, u32[]{:S(2)}) %copy-start.2) | copy-done | bytes 2072
  3.9 0.0 copy-start.3
  3.9 0.7 %copy-done.3 = s32[2,8]{1,0:T(2,128)S(1)} copy-done((s32[2,8]{1,0:T(2,128)S(1)}, s32[2,8]{1,0:T(2,128)}, u32[]{:S(2)}) %copy-start.3) | copy-done | bytes 88
  4.5 0.0 copy-start.4
  4.5 0.7 %copy-done.4 = s32[16]{0:T(128)S(1)} copy-done((s32[16]{0:T(128)S(1)}, s32[16]{0:T(128)}, u32[]{:S(2)}) %copy-start.4) | copy-done | bytes 88
  5.2 36.1 %shard_map.68 = (bf16[2,2,256,256]{3,2,1,0:T(8,128)(2,1)S(1)}, f32[2,256]{1,0:T(2,128)S(1)}) custom-call(s32[2,8]{1,0:T(2,128)S(1)} %copy-done.3, s32[16]{0:T(128)S(1)} %copy-done.4, bf16[2,8,256,256]{3,2,1,0:T(8,128)(2,1)S(1)} %copy-done, bf16[2,1,256,256]{3,2,1,0:T(8,128)(2,1)S(1)} %copy-done.1, f32[2,256]{1,0:T(2,128)S(1)} %copy-done.2), custom_call_target="tpu_custom_call" | custom-call | flops 1073741824 | bytes 4194304 | tf_op jit(solution)/shard_map/pallas_call | solution.py:295
  41.3 0.8 %copy.9 = bf16[2,2,256,256]{3,2,1,0:T(8,128)(2,1)} copy(bf16[2,2,256,256]{3,2,1,0:T(8,128)(2,1)S(1)} %get-tuple-element.4) | data formatting | bytes 1048576
  42.1 0.6 %copy.10 = f32[2,256]{1,0:T(2,128)} copy(f32[2,256]{1,0:T(2,128)S(1)} %get-tuple-element.5) | data formatting | bytes 4096
Async XLA Ops:
  0.6 1.6 %copy-start = (bf16[2,8,256,256]{3,2,1,0:T(8,128)(2,1)S(1)}, bf16[2,8,256,256]{3,2,1,0:T(8,128)(2,1)}, u32[]{:S(2)}) copy-start(bf16[2,8,256,256]{3,2,1,0:T(8,128)(2,1)} %tiles.1) | copy-start | bytes 6291460
  2.2 0.9 %copy-start.1 = (bf16[2,1,256,256]{3,2,1,0:T(8,128)(2,1)S(1)}, bf16[2,1,256,256]{3,2,1,0:T(8,128)(2,1)}, u32[]{:S(2)}) copy-start(bf16[2,1,256,256]{3,2,1,0:T(8,128)(2,1)} %panel.1) | copy-start | bytes 786436
  3.2 0.7 %copy-start.2 = (f32[2,256]{1,0:T(2,128)S(1)}, f32[2,256]{1,0:T(2,128)}, u32[]{:S(2)}) copy-start(f32[2,256]{1,0:T(2,128)} %diag.1) | copy-start | bytes 6148
  3.9 0.7 %copy-start.3 = (s32[2,8]{1,0:T(2,128)S(1)}, s32[2,8]{1,0:T(2,128)}, u32[]{:S(2)}) copy-start(s32[2,8]{1,0:T(2,128)} %structure.1) | copy-start | bytes 196
  4.5 0.7 %copy-start.4 = (s32[16]{0:T(128)S(1)}, s32[16]{0:T(128)}, u32[]{:S(2)}) copy-start(s32[16]{0:T(128)} %block_slot.1) | copy-start | bytes 196

commit v2 on v1

--- a/solution.py
+++ b/solution.py
@@ -25,8 +25,8 @@
 
 
 def kernel(
-    line, wide, structure, block_slot, tiles, panel, diag, sigma, variance,
-    full, acc, part, parts, *rest,
+    line, wide, structure_in, block_slot_in, tiles, panel, diag_in, sigma_out, variance,
+    structure, block_slot, diag, list_sem, sigma, sigma_sem, full, acc, part, parts, *rest,
 ):
     supers = structure.shape[0]
     positions = structure.shape[1]
@@ -51,13 +51,33 @@
         return zz * wide + yy
 
     barrier = pltpu.get_barrier_semaphore()
-    for shift in range(1, count):
-        pl.semaphore_signal(
-            barrier, inc=1, device_id={"prow": lax.rem(me + shift, count)},
-            device_id_type=MESH,
-        )
-    pl.semaphore_signal(barrier, inc=1, device_id={"pcol": 1 - core}, device_id_type=MESH)
-    pl.semaphore_wait(barrier, count)
+    up, down = at(z + 1, y), at(z - 1, y)
+    has_up, has_down = z + 1 < line, z >= 1
+
+    def greet(place):
+        pl.semaphore_signal(barrier, inc=1, device_id=place, device_id_type=MESH)
+
+    @pl.when(has_up)
+    def _():
+        greet({"prow": up})
+
+    @pl.when(has_down)
+    def _():
+        greet({"prow": down})
+
+    if wide == 2:
+        greet({"prow": sibling})
+    greet({"pcol": 1 - core})
+    lists = [
+        pltpu.make_async_copy(structure_in, structure, list_sem.at[0]),
+        pltpu.make_async_copy(block_slot_in, block_slot, list_sem.at[1]),
+    ]
+    lists.append(pltpu.make_async_copy(diag_in, diag, list_sem.at[2]))
+    for copy in lists:
+        copy.start()
+    pl.semaphore_wait(
+        barrier, wide + jnp.where(has_up, 1, 0) + jnp.where(has_down, 1, 0)
+    )
 
     def send(s, source, kind, to, own=False):
         return pltpu.make_async_remote_copy(
@@ -72,9 +92,6 @@
     def arrive(s, source):
         send(s, source, UP, me).wait_recv()
 
-    up, down = at(z + 1, y), at(z - 1, y)
-    has_up, has_down = z + 1 < line, z >= 1
-
     for s in range(supers):
         if wide == 2:
             send(s, me, ACROSS, sibling, True).start()
@@ -123,6 +140,8 @@
         return zz != z + 1 - 2 * (z % 2)
 
     def flush():
+        for copy in lists:
+            copy.wait()
         for s in range(supers):
             own[s].wait()
         keep.wait()
@@ -194,6 +213,11 @@
     if wide == 2:
         extra = send(last, sibling, EXTRA, twin)
         extra.start()
+
+    written = [
+        pltpu.make_async_copy(sigma.at[s], sigma_out.at[s], sigma_sem.at[s])
+        for s in range(supers)
+    ]
 
     def finish(s):
         total = jnp.zeros((1, width), jnp.float32)
@@ -217,6 +241,7 @@
                 arrive(s, at(z + 1 - 2 * (z % 2), 1 - y))
                 add(s, at(z + 1 - 2 * (z % 2), 1 - y))
         finish(s)
+        written[s].start()
 
     def share(shift):
         to = lax.rem(me + shift, count)
@@ -280,6 +305,8 @@
         share(shift).wait()
         total = total - parts[shift]
     variance[...] = total
+    for s in range(supers):
+        written[s].wait()
 
 
 def per_device(line, wide, inverse_tiles, panel_blocks, diag_inverse, structure, block_slot):
@@ -289,8 +316,7 @@
     bf16, f32 = jnp.bfloat16, jnp.float32
     dma = pltpu.SemaphoreType.DMA
     whole = pl.BlockSpec(memory_space=pltpu.VMEM)
-    scalars = pl.BlockSpec(memory_space=pltpu.SMEM)
-    anywhere = pl.BlockSpec(memory_space=pl.ANY)
+    outside = pl.BlockSpec(memory_space=pltpu.HBM)
     flops = 2 * supers * rows * tile * width * tile * structure.shape[1]
     return pl.pallas_call(
         functools.partial(kernel, line, wide),
@@ -298,9 +324,15 @@
             jax.ShapeDtypeStruct((supers, rows, tile, width), bf16),
             jax.ShapeDtypeStruct((supers, width), f32),
         ),
-        in_specs=[scalars, scalars, anywhere, anywhere, whole],
-        out_specs=(whole, whole),
+        in_specs=[outside] * 5,
+        out_specs=(outside, whole),
         scratch_shapes=[
+            pltpu.SMEM(structure.shape, structure.dtype),
+            pltpu.SMEM(block_slot.shape, block_slot.dtype),
+            pltpu.VMEM(diag_inverse.shape, f32),
+            dma((3,)),
+            pltpu.VMEM((supers, rows, tile, width), bf16),
+            dma((supers,)),
             pltpu.VMEM((rows, 2 * columns, tile, tile), bf16),
             pltpu.VMEM((supers, rows * tile, width), f32),
             pltpu.VMEM((supers, width), f32),
@@ -316,7 +348,7 @@
             dma((count,)),
         ],
         compiler_params=pltpu.CompilerParams(
-            collective_id=0, has_side_effects=True, vmem_limit_bytes=48 * 2**20
+            collective_id=0, has_side_effects=True, vmem_limit_bytes=60 * 2**20
         ),
         cost_estimate=pl.CostEstimate(
             flops=flops, bytes_accessed=4 * inverse_tiles.size, transcendentals=0

time: 42.9 us -> 39.4 us (0.918)
  local copies, waits for them, and re-layouts: 5.92 us -> 3.12 us
  Pallas kernels: 36.1 us -> 35.5 us
    unnamed x12 -> x2, local copies, waits for them, and re-layouts: 5.92 us -> 3.12 us
    pallas_call x1, Pallas kernels: 36.1 us -> 35.5 us  [per_device(): pl.pallas_call(functools.partial(kernel, line, wide), out_shape=(jax.Shap...]
where the time goes in v2:
time: 39.4 us; the launch traced here: 39.3 us
  Pallas kernels  35.5 us (90%)
  local copies, waits for them, and re-layouts  3.12 us (8%)
  between operations  0.64 us (2%)
    pallas_call x1, Pallas kernels, per_device(): pl.pallas_call(functools.partial(kernel, line, wide), out_shape=(jax.Shap...  35.5 us
    unnamed x2, local copies, waits for them, and re-layouts  3.12 us

profile of v2, /device:TPU:0, one launch (start us, length us, event | category | flops | bytes accessed | tf_op | source)
XLA Modules:
  0.0 39.3 jit_solution(12705407088865039096)
XLA Ops:
  0.6 35.5 %shard_map.68 = (bf16[2,2,256,256]{3,2,1,0:T(8,128)(2,1)}, f32[2,256]{1,0:T(2,128)}) custom-call(s32[2,8]{1,0:T(2,128)} %structure_in.1, s32[16]{0:T(128)} %block_slot_in.1, bf16[2,8,256,256]{3,2,1,0:T(8,128)(2,1)} %tiles.1, bf16[2,1,256,256]{3,2,1,0:T(8,128)(2,1)} %panel.1, f32[2,256]{1,0:T(2,128)} %diag_in.1), custom_call_target="tpu_custom_call" | custom-call | flops 1073741824 | bytes 4194304 | tf_op jit(solution)/shard_map/pallas_call | solution.py:321
  36.1 1.9 %copy.9 = bf16[2,2,256,256]{3,2,1,0:T(8,128)(2,1)} copy(bf16[2,2,256,256]{3,2,1,0:T(8,128)(2,1)} %get-tuple-element.4) | data formatting | bytes 1048576
  38.0 1.3 %copy.10 = f32[2,256]{1,0:T(2,128)} copy(f32[2,256]{1,0:T(2,128)} %get-tuple-element.5) | data formatting | bytes 4096

commit v3 on v2

--- a/solution.py
+++ b/solution.py
@@ -9,6 +9,7 @@
 
 MESH = pl.DeviceIdType.MESH
 UP, DOWN, ACROSS, EXTRA = range(4)
+PIECES = 2
 
 
 def grid_of(mesh):
@@ -25,8 +26,8 @@
 
 
 def kernel(
-    line, wide, structure_in, block_slot_in, tiles, panel, diag_in, sigma_out, variance,
-    structure, block_slot, diag, list_sem, sigma, sigma_sem, full, acc, part, parts, *rest,
+    line, wide, structure_in, block_slot_in, tiles, panel, diag_in, sigma, variance,
+    structure, block_slot, diag, list_sem, full, acc, part, parts, *rest,
 ):
     supers = structure.shape[0]
     positions = structure.shape[1]
@@ -46,6 +47,8 @@
     sibling = z * wide + (wide - 1 - y)
     twin = (z + 1 - 2 * (z % 2)) * wide + y
     last = supers - 1
+    depth = tile // PIECES
+    chunks = [(s, h) for s in range(supers) for h in range(PIECES)]
 
     def at(zz, yy):
         return zz * wide + yy
@@ -79,30 +82,33 @@
         barrier, wide + jnp.where(has_up, 1, 0) + jnp.where(has_down, 1, 0)
     )
 
-    def send(s, source, kind, to, own=False):
+    def send(c, source, kind, to, own=False):
+        s, h = c
+        piece = pl.ds(h * depth, depth)
+        target = panels[s].at[source, :, piece]
         return pltpu.make_async_remote_copy(
-            src_ref=panel.at[s] if own else panels[s].at[source],
-            dst_ref=panels[s].at[source],
-            send_sem=send_sem.at[kind, s, source],
-            recv_sem=recv_sem.at[s, source],
+            src_ref=panel.at[s, :, piece] if own else target,
+            dst_ref=target,
+            send_sem=send_sem.at[kind, s * PIECES + h, source],
+            recv_sem=recv_sem.at[s * PIECES + h, source],
             device_id={"prow": to},
             device_id_type=MESH,
         )
 
-    def arrive(s, source):
-        send(s, source, UP, me).wait_recv()
-
-    for s in range(supers):
+    def arrive(c, source):
+        send(c, source, UP, me).wait_recv()
+
+    for c in chunks:
         if wide == 2:
-            send(s, me, ACROSS, sibling, True).start()
+            send(c, me, ACROSS, sibling, True).start()
 
         @pl.when(has_up)
         def _():
-            send(s, me, UP, up, True).start()
+            send(c, me, UP, up, True).start()
 
         @pl.when(has_down)
         def _():
-            send(s, me, DOWN, down, True).start()
+            send(c, me, DOWN, down, True).start()
 
     swap = pltpu.make_async_remote_copy(
         src_ref=tiles,
@@ -148,76 +154,97 @@
         swap.wait_recv()
         for s in range(supers):
             add(s, me)
+            add_both(s, 1)
+
+    def pass_on(c, d):
+        above, below = z + d, z - d
+
+        @pl.when(above < line)
+        def _():
+            arrive(c, at(above, y))
+
+            @pl.when(has_down)
+            def _():
+                send(c, at(above, y), DOWN, down).start()
+
+            if wide == 2:
+                @pl.when(crosses(c[0], above))
+                def _():
+                    send(c, at(above, y), ACROSS, sibling).start()
+
+        @pl.when(below >= 0)
+        def _():
+            arrive(c, at(below, y))
+
+            @pl.when(has_up)
+            def _():
+                send(c, at(below, y), UP, up).start()
+
+            if wide == 2:
+                @pl.when(crosses(c[0], below))
+                def _():
+                    send(c, at(below, y), ACROSS, sibling).start()
+
+    def add_both(s, d):
+        above, below = z + d, z - d
+
+        @pl.when(above < line)
+        def _():
+            add(s, at(above, y))
+
+        @pl.when(below >= 0)
+        def _():
+            add(s, at(below, y))
 
     def step(d, _):
-        above, below = z + d, z - d
         for s in range(supers):
-            @pl.when(above < line)
-            def _():
-                arrive(s, at(above, y))
-
-                @pl.when(has_down)
-                def _():
-                    send(s, at(above, y), DOWN, down).start()
-
-                if wide == 2:
-                    @pl.when(crosses(s, above))
-                    def _():
-                        send(s, at(above, y), ACROSS, sibling).start()
-
-            @pl.when(below >= 0)
-            def _():
-                arrive(s, at(below, y))
-
-                @pl.when(has_up)
-                def _():
-                    send(s, at(below, y), UP, up).start()
-
-                if wide == 2:
-                    @pl.when(crosses(s, below))
-                    def _():
-                        send(s, at(below, y), ACROSS, sibling).start()
-
-            if s == 0:
+            for h in range(PIECES):
+                pass_on((s, h), d)
+            if s == last:
                 @pl.when(d == 1)
                 def _():
                     flush()
 
-            @pl.when(above < line)
-            def _():
-                add(s, at(above, y))
-
-            @pl.when(below >= 0)
-            def _():
-                add(s, at(below, y))
-
-            if wide == 2:
-                across(s, d - 1)
+            @pl.when(d > 1)
+            def _():
+                add_both(s, d)
         return 0
+
+    lax.fori_loop(1, line, step, 0)
+
+    def arrive_all(s, source):
+        for h in range(PIECES):
+            arrive((s, h), source)
 
     def across(s, d):
         above, below = z + d, z - d
 
         @pl.when((above < line) & crosses(s, above))
         def _():
-            arrive(s, at(above, 1 - y))
+            arrive_all(s, at(above, 1 - y))
             add(s, at(above, 1 - y))
 
-        @pl.when((below >= 0) & crosses(s, below) & (d > 0))
-        def _():
-            arrive(s, at(below, 1 - y))
+        @pl.when((below >= 0) & crosses(s, below))
+        def _():
+            arrive_all(s, at(below, 1 - y))
             add(s, at(below, 1 - y))
 
-    lax.fori_loop(1, line, step, 0)
-
     if wide == 2:
-        extra = send(last, sibling, EXTRA, twin)
-        extra.start()
-
-    written = [
-        pltpu.make_async_copy(sigma.at[s], sigma_out.at[s], sigma_sem.at[s])
-        for s in range(supers)
-    ]
+        extra = [send((last, h), sibling, EXTRA, twin) for h in range(PIECES)]
+        for h in range(PIECES):
+            arrive((last, h), sibling)
+            extra[h].start()
+        for s in range(supers):
+            if s != last:
+                arrive_all(s, sibling)
+            add(s, sibling)
+
+        def later(d, _):
+            for s in range(supers):
+                across(s, d)
+            return 0
+
+        lax.fori_loop(1, line - 1, later, 0)
 
     def finish(s):
         total = jnp.zeros((1, width), jnp.float32)
@@ -238,10 +265,9 @@
         if wide == 2:
             across(s, line - 1)
             if s == last:
-                arrive(s, at(z + 1 - 2 * (z % 2), 1 - y))
+                arrive_all(s, at(z + 1 - 2 * (z % 2), 1 - y))
                 add(s, at(z + 1 - 2 * (z % 2), 1 - y))
         finish(s)
-        written[s].start()
 
     def share(shift):
         to = lax.rem(me + shift, count)
@@ -257,47 +283,48 @@
     for shift in range(1, count):
         share(shift).start()
 
-    for s in range(supers):
+    for c in chunks:
         if wide == 2:
-            send(s, me, ACROSS, sibling, True).wait_send()
+            send(c, me, ACROSS, sibling, True).wait_send()
 
         @pl.when(has_up)
         def _():
-            send(s, me, UP, up, True).wait_send()
+            send(c, me, UP, up, True).wait_send()
 
         @pl.when(has_down)
         def _():
-            send(s, me, DOWN, down, True).wait_send()
+            send(c, me, DOWN, down, True).wait_send()
 
     def left(d, _):
         above, below = z + d, z - d
-        for s in range(supers):
+        for c in chunks:
             @pl.when(above < line)
             def _():
                 @pl.when(has_down)
                 def _():
-                    send(s, at(above, y), DOWN, down).wait_send()
+                    send(c, at(above, y), DOWN, down).wait_send()
 
                 if wide == 2:
-                    @pl.when(crosses(s, above))
+                    @pl.when(crosses(c[0], above))
                     def _():
-                        send(s, at(above, y), ACROSS, sibling).wait_send()
+                        send(c, at(above, y), ACROSS, sibling).wait_send()
 
             @pl.when(below >= 0)
             def _():
                 @pl.when(has_up)
                 def _():
-                    send(s, at(below, y), UP, up).wait_send()
+                    send(c, at(below, y), UP, up).wait_send()
 
                 if wide == 2:
-                    @pl.when(crosses(s, below))
+                    @pl.when(crosses(c[0], below))
                     def _():
-                        send(s, at(below, y), ACROSS, sibling).wait_send()
+                        send(c, at(below, y), ACROSS, sibling).wait_send()
         return 0
 
     lax.fori_loop(1, line, left, 0)
     if wide == 2:
-        extra.wait_send()
+        for h in range(PIECES):
+            extra[h].wait_send()
     swap.wait_send()
 
     total = diag[...] - part[...]
@@ -305,8 +332,6 @@
         share(shift).wait()
         total = total - parts[shift]
     variance[...] = total
-    for s in range(supers):
-        written[s].wait()
 
 
 def per_device(line, wide, inverse_tiles, panel_blocks, diag_inverse, structure, block_slot):
@@ -321,26 +346,24 @@
     return pl.pallas_call(
         functools.partial(kernel, line, wide),
         out_shape=(
-            jax.ShapeDtypeStruct((supers, rows, tile, width), bf16),
-            jax.ShapeDtypeStruct((supers, width), f32),
+            pltpu.VMEM((supers, rows, tile, width), bf16),
+            pltpu.VMEM((supers, width), f32),
         ),
         in_specs=[outside] * 5,
-        out_specs=(outside, whole),
+        out_specs=(whole, whole),
         scratch_shapes=[
             pltpu.SMEM(structure.shape, structure.dtype),
             pltpu.SMEM(block_slot.shape, block_slot.dtype),
             pltpu.VMEM(diag_inverse.shape, f32),
             dma((3,)),
-            pltpu.VMEM((supers, rows, tile, width), bf16),
-            dma((supers,)),
             pltpu.VMEM((rows, 2 * columns, tile, tile), bf16),
             pltpu.VMEM((supers, rows * tile, width), f32),
             pltpu.VMEM((supers, width), f32),
             pltpu.VMEM((count, supers, width), f32),
             *[pltpu.VMEM((count, held, tile, width), bf16) for _ in range(supers)],
             dma((supers,)),
-            dma((4, supers, count)),
-            dma((supers, count)),
+            dma((4, supers * PIECES, count)),
+            dma((supers * PIECES, count)),
             dma,
             dma,
             dma,

time: 39.4 us -> 36.3 us (0.921)
  local copies, waits for them, and re-layouts: 3.12 us -> 1.37 us
  Pallas kernels: 35.5 us -> 34.1 us
    unnamed x2, local copies, waits for them, and re-layouts: 3.12 us -> 1.37 us
    pallas_call x1, Pallas kernels: 35.5 us -> 34.1 us  [per_device(): pl.pallas_call(functools.partial(kernel, line, wide), out_shape=(pltpu.VM...]
where the time goes in v3:
time: 36.3 us; the launch traced here: 36.1 us
  Pallas kernels  34.1 us (94%)
  local copies, waits for them, and re-layouts  1.37 us (4%)
  between operations  0.64 us (2%)
    pallas_call x1, Pallas kernels, per_device(): pl.pallas_call(functools.partial(kernel, line, wide), out_shape=(pltpu.VM...  34.1 us
    unnamed x2, local copies, waits for them, and re-layouts  1.37 us

profile of v3, /device:TPU:0, one launch (start us, length us, event | category | flops | bytes accessed | tf_op | source)
XLA Modules:
  0.0 36.1 jit_solution(5464118922614688287)
XLA Ops:
  0.6 34.1 %shard_map.68 = (bf16[2,2,256,256]{3,2,1,0:T(8,128)(2,1)S(1)}, f32[2,256]{1,0:T(2,128)S(1)}) custom-call(s32[2,8]{1,0:T(2,128)} %structure_in.1, s32[16]{0:T(128)} %block_slot_in.1, bf16[2,8,256,256]{3,2,1,0:T(8,128)(2,1)} %tiles.1, bf16[2,1,256,256]{3,2,1,0:T(8,128)(2,1)} %panel.1, f32[2,256]{1,0:T(2,128)} %diag_in.1), custom_call_target="tpu_custom_call" | custom-call | flops 1073741824 | bytes 4194304 | tf_op jit(solution)/shard_map/pallas_call | solution.py:346
  34.8 0.8 %copy.9 = bf16[2,2,256,256]{3,2,1,0:T(8,128)(2,1)} copy(bf16[2,2,256,256]{3,2,1,0:T(8,128)(2,1)S(1)} %get-tuple-element.2) | data formatting | bytes 1048576
  35.6 0.6 %copy.10 = f32[2,256]{1,0:T(2,128)} copy(f32[2,256]{1,0:T(2,128)S(1)} %get-tuple-element.3) | data formatting | bytes 4096

commit v4 on v3

--- a/solution.py
+++ b/solution.py
@@ -9,7 +9,7 @@
 
 MESH = pl.DeviceIdType.MESH
 UP, DOWN, ACROSS, EXTRA = range(4)
-PIECES = 2
+PIECES = 4
 
 
 def grid_of(mesh):
@@ -47,6 +47,7 @@
     sibling = z * wide + (wide - 1 - y)
     twin = (z + 1 - 2 * (z % 2)) * wide + y
     last = supers - 1
+    first = min(2, line - 1)
     depth = tile // PIECES
     chunks = [(s, h) for s in range(supers) for h in range(PIECES)]
 
@@ -154,7 +155,8 @@
         swap.wait_recv()
         for s in range(supers):
             add(s, me)
-            add_both(s, 1)
+            for d in range(1, first + 1):
+                add_both(s, d)
 
     def pass_on(c, d):
         above, below = z + d, z - d
@@ -201,11 +203,11 @@
             for h in range(PIECES):
                 pass_on((s, h), d)
             if s == last:
-                @pl.when(d == 1)
+                @pl.when(d == first)
                 def _():
                     flush()
 
-            @pl.when(d > 1)
+            @pl.when(d > first)
             def _():
                 add_both(s, d)
         return 0

time: 36.3 us -> 37.7 us (1.039)
  Pallas kernels: 34.1 us -> 35.5 us
    pallas_call x1, Pallas kernels: 34.1 us -> 35.5 us  [per_device(): pl.pallas_call(functools.partial(kernel, line, wide), out_shape=(pltpu.VM...]
where the time goes in v4:
time: 37.7 us; the launch traced here: 37.5 us
  Pallas kernels  35.5 us (94%)
  local copies, waits for them, and re-layouts  1.37 us (4%)
  between operations  0.64 us (2%)
    pallas_call x1, Pallas kernels, per_device(): pl.pallas_call(functools.partial(kernel, line, wide), out_shape=(pltpu.VM...  35.5 us
    unnamed x2, local copies, waits for them, and re-layouts  1.37 us

profile of v4, /device:TPU:0, one launch (start us, length us, event | category | flops | bytes accessed | tf_op | source)
XLA Modules:
  0.0 37.5 jit_solution(15692545981081000404)
XLA Ops:
  0.6 35.5 %shard_map.68 = (bf16[2,2,256,256]{3,2,1,0:T(8,128)(2,1)S(1)}, f32[2,256]{1,0:T(2,128)S(1)}) custom-call(s32[2,8]{1,0:T(2,128)} %structure_in.1, s32[16]{0:T(128)} %block_slot_in.1, bf16[2,8,256,256]{3,2,1,0:T(8,128)(2,1)} %tiles.1, bf16[2,1,256,256]{3,2,1,0:T(8,128)(2,1)} %panel.1, f32[2,256]{1,0:T(2,128)} %diag_in.1), custom_call_target="tpu_custom_call" | custom-call | flops 1073741824 | bytes 4194304 | tf_op jit(solution)/shard_map/pallas_call | solution.py:348
  36.2 0.8 %copy.9 = bf16[2,2,256,256]{3,2,1,0:T(8,128)(2,1)} copy(bf16[2,2,256,256]{3,2,1,0:T(8,128)(2,1)S(1)} %get-tuple-element.2) | data formatting | bytes 1048576
  37.0 0.6 %copy.10 = f32[2,256]{1,0:T(2,128)} copy(f32[2,256]{1,0:T(2,128)S(1)} %get-tuple-element.3) | data formatting | bytes 4096

commit v5 on v3

--- a/solution.py
+++ b/solution.py
@@ -229,6 +229,29 @@
             arrive_all(s, at(below, 1 - y))
             add(s, at(below, 1 - y))
 
+    for c in chunks:
+        @pl.when(has_up)
+        def _():
+            send(c, me, UP, up, True).wait_send()
+
+        @pl.when(has_down)
+        def _():
+            send(c, me, DOWN, down, True).wait_send()
+
+    def left_line(d, _):
+        above, below = z + d, z - d
+        for c in chunks:
+            @pl.when((above < line) & has_down)
+            def _():
+                send(c, at(above, y), DOWN, down).wait_send()
+
+            @pl.when((below >= 0) & has_up)
+            def _():
+                send(c, at(below, y), UP, up).wait_send()
+        return 0
+
+    lax.fori_loop(1, line, left_line, 0)
+
     if wide == 2:
         extra = [send((last, h), sibling, EXTRA, twin) for h in range(PIECES)]
         for h in range(PIECES):
@@ -283,45 +306,23 @@
     for shift in range(1, count):
         share(shift).start()
 
-    for c in chunks:
-        if wide == 2:
+    if wide == 2:
+        for c in chunks:
             send(c, me, ACROSS, sibling, True).wait_send()
 
-        @pl.when(has_up)
-        def _():
-            send(c, me, UP, up, True).wait_send()
-
-        @pl.when(has_down)
-        def _():
-            send(c, me, DOWN, down, True).wait_send()
-
-    def left(d, _):
-        above, below = z + d, z - d
-        for c in chunks:
-            @pl.when(above < line)
-            def _():
-                @pl.when(has_down)
-                def _():
-                    send(c, at(above, y), DOWN, down).wait_send()
-
-                if wide == 2:
-                    @pl.when(crosses(c[0], above))
-                    def _():
-                        send(c, at(above, y), ACROSS, sibling).wait_send()
-
-            @pl.when(below >= 0)
-            def _():
-                @pl.when(has_up)
-                def _():
-                    send(c, at(below, y), UP, up).wait_send()
-
-                if wide == 2:
-                    @pl.when(crosses(c[0], below))
-                    def _():
-                        send(c, at(below, y), ACROSS, sibling).wait_send()
-        return 0
-
-    lax.fori_loop(1, line, left, 0)
+        def left_across(d, _):
+            above, below = z + d, z - d
+            for c in chunks:
+                @pl.when((above < line) & crosses(c[0], above))
+                def _():
+                    send(c, at(above, y), ACROSS, sibling).wait_send()
+
+                @pl.when((below >= 0) & crosses(c[0], below))
+                def _():
+                    send(c, at(below, y), ACROSS, sibling).wait_send()
+            return 0
+
+        lax.fori_loop(1, line, left_across, 0)
     if wide == 2:
         for h in range(PIECES):
             extra[h].wait_send()

time: 36.3 us -> 35.8 us (0.986)
  Pallas kernels: 34.1 us -> 33.6 us
    pallas_call x1, Pallas kernels: 34.1 us -> 33.6 us  [per_device(): pl.pallas_call(functools.partial(kernel, line, wide), out_shape=(pltpu.VM...]
where the time goes in v5:
time: 35.8 us; the launch traced here: 35.6 us
  Pallas kernels  33.6 us (94%)
  local copies, waits for them, and re-layouts  1.37 us (4%)
  between operations  0.64 us (2%)
    pallas_call x1, Pallas kernels, per_device(): pl.pallas_call(functools.partial(kernel, line, wide), out_shape=(pltpu.VM...  33.6 us
    unnamed x2, local copies, waits for them, and re-layouts  1.37 us

profile of v5, /device:TPU:0, one launch (start us, length us, event | category | flops | bytes accessed | tf_op | source)
XLA Modules:
  0.0 35.6 jit_solution(16974358971309163533)
XLA Ops:
  0.6 33.6 %shard_map.68 = (bf16[2,2,256,256]{3,2,1,0:T(8,128)(2,1)S(1)}, f32[2,256]{1,0:T(2,128)S(1)}) custom-call(s32[2,8]{1,0:T(2,128)} %structure_in.1, s32[16]{0:T(128)} %block_slot_in.1, bf16[2,8,256,256]{3,2,1,0:T(8,128)(2,1)} %tiles.1, bf16[2,1,256,256]{3,2,1,0:T(8,128)(2,1)} %panel.1, f32[2,256]{1,0:T(2,128)} %diag_in.1), custom_call_target="tpu_custom_call" | custom-call | flops 1073741824 | bytes 4194304 | tf_op jit(solution)/shard_map/pallas_call | solution.py:347
  34.3 0.8 %copy.9 = bf16[2,2,256,256]{3,2,1,0:T(8,128)(2,1)} copy(bf16[2,2,256,256]{3,2,1,0:T(8,128)(2,1)S(1)} %get-tuple-element.2) | data formatting | bytes 1048576
  35.1 0.6 %copy.10 = f32[2,256]{1,0:T(2,128)} copy(f32[2,256]{1,0:T(2,128)S(1)} %get-tuple-element.3) | data formatting | bytes 4096
